TPU v7x, 512 devices: a whole 4x4x16 slice. The times are simulated.
512 devices in a mesh: dp: 32 (over z, core), fsdp: 16 (over y, x).
Axes of the slice: x: 4, y: 4, z: 16, core: 2. Of those that a mesh axis runs over, the one named last changes fastest.
Arguments:
- tile: bfloat16 [65536, 2048], P(('dp', 'fsdp')), may hold values from -6 to 6
- cotangent: bfloat16 [65536, 2048], P(('dp', 'fsdp')), may hold values from -6 to 6
- combine: float32 [65536], P(('dp', 'fsdp')), may hold values from 0.05 to 0.6
- valid: int32 [512], P(('dp', 'fsdp')), may hold values from 1 to 128, as said below
- w_gate: bfloat16 [2048, 768], P('fsdp'), may hold values from -0.125 to 0.125
- w_up: bfloat16 [2048, 768], P('fsdp'), may hold values from -0.125 to 0.125
- w_down: bfloat16 [768, 2048], P(None, 'fsdp'), may hold values from -0.21875 to 0.21875
Outputs:
- output: bfloat16 [65536, 2048], P(('dp', 'fsdp'))
- tile_grad: bfloat16 [65536, 2048], P(('dp', 'fsdp'))
- combine_grad: float32 [65536], P(('dp', 'fsdp'))
- grad_gate: float32 [2048, 768], P('fsdp', 'dp')
- grad_up: float32 [2048, 768], P('fsdp', 'dp')
- grad_down: float32 [768, 2048], P('dp', 'fsdp')
Inputs may be any that keep to these rules, and one draw needn't show every extreme that they name: `valid`: some device's tile is full in every draw.
All inputs are finite; a program needn't handle non-finite values.
Results may differ from a plain program's by a relative error of at most 0.0058.
Values may be sent and summed in bfloat16 or wider, within the bound.
A program may use at most 64 MiB of HBM per device.

v0:
```python
import math

import jax
import jax.numpy as jnp
from jax import lax
from jax.sharding import PartitionSpec as P


def contract_last(left, right):
    return lax.dot_general(
        left, right, (((1,), (1,)), ((), ())), preferred_element_type=jnp.float32
    )


def contract_first(left, right):
    return lax.dot_general(
        left, right, (((0,), (0,)), ((), ())), preferred_element_type=jnp.float32
    )


def on_device(tile, cotangent, combine, valid, w_gate, w_up, w_down):
    rows_here = tile.shape[0]
    rows_total = rows_here * lax.axis_size("dp") * lax.axis_size("fsdp")
    keep = (jnp.arange(rows_here) < valid[0]).astype(jnp.float32)[:, None]
    columns = tile
    gate = jnp.dot(
        columns,
        lax.all_gather(w_gate, "fsdp", axis=0, tiled=True),
        preferred_element_type=jnp.float32,
    )
    up = jnp.dot(
        columns,
        lax.all_gather(w_up, "fsdp", axis=0, tiled=True),
        preferred_element_type=jnp.float32,
    )
    hidden = (jax.nn.silu(gate) * up).astype(jnp.bfloat16)
    hidden_all = lax.all_gather(hidden, "fsdp", axis=0, tiled=True)
    partial_out = jnp.dot(hidden_all, w_down, preferred_element_type=jnp.float32)
    expert_out = lax.all_to_all(partial_out, "fsdp", split_axis=0, concat_axis=1, tiled=True)
    weight = keep * combine[:, None]
    output = (weight * expert_out).astype(jnp.bfloat16)
    width_scale = 1.0 / math.sqrt(tile.shape[1])
    combine_grad = (
        keep[:, 0] * jnp.sum(cotangent.astype(jnp.float32) * expert_out, axis=1) * width_scale
    )
    dy = (weight * cotangent.astype(jnp.float32)).astype(jnp.bfloat16)
    tile_cols, dy_cols = (
        lax.all_to_all(tile, "fsdp", split_axis=1, concat_axis=0, tiled=True),
        lax.all_to_all(dy, "fsdp", split_axis=1, concat_axis=0, tiled=True),
    )
    factor = 1.0 / math.sqrt(rows_total)
    down_term = contract_first(hidden_all, dy_cols) * factor
    grad_down = lax.psum_scatter(down_term, "dp", scatter_dimension=0, tiled=True)
    columns = dy
    dhidden = contract_last(columns, lax.all_gather(w_down, "fsdp", axis=1, tiled=True))
    sigma = jax.nn.sigmoid(gate)
    dgate = (dhidden * up * sigma * (1.0 + gate * (1.0 - sigma))).astype(jnp.bfloat16)
    dup = (dhidden * gate * sigma).astype(jnp.bfloat16)
    dgate_all, dup_all = (
        lax.all_gather(dgate, "fsdp", axis=0, tiled=True),
        lax.all_gather(dup, "fsdp", axis=0, tiled=True),
    )
    partial_in = (contract_last(dgate_all, w_gate) + contract_last(dup_all, w_up)).astype(
        jnp.bfloat16
    )
    tile_grad = lax.all_to_all(partial_in, "fsdp", split_axis=0, concat_axis=1, tiled=True)
    gate_term = contract_first(tile_cols, dgate_all) * factor
    up_term = contract_first(tile_cols, dup_all) * factor
    grad_gate, grad_up = (
        lax.psum_scatter(gate_term, "dp", scatter_dimension=1, tiled=True),
        lax.psum_scatter(up_term, "dp", scatter_dimension=1, tiled=True),
    )
    return (output, tile_grad, combine_grad, grad_gate, grad_up, grad_down)


def solution(mesh):
    in_specs = (
        P(("dp", "fsdp"), None),
        P(("dp", "fsdp"), None),
        P(("dp", "fsdp")),
        P(("dp", "fsdp")),
        P("fsdp", None),
        P("fsdp", None),
        P(None, "fsdp"),
    )
    out_specs = (
        P(("dp", "fsdp"), None),
        P(("dp", "fsdp"), None),
        P(("dp", "fsdp")),
        P("fsdp", "dp"),
        P("fsdp", "dp"),
        P("dp", "fsdp"),
    )
    return jax.shard_map(
        on_device, mesh=mesh, in_specs=in_specs, out_specs=out_specs, check_vma=False
    )
```

profile of v0, /device:TPU:6, one launch (start us, length us, event | category | flops | bytes accessed | tf_op | source)
XLA Modules:
  0.0 748.3 jit_solution(10309027352364897478)
XLA Ops:
  13.0 65.0 %all-gather.7.cloned.1.call-done = bf16[2048,768]{1,0:T(8,128)(2,1)} async-done(((bf16[128,768]{1,0:T(8,128)(2,1)}), bf16[2048,768]{1,0:T(8,128)(2,1)}) %all-gather.7.cloned.1.call-update) | async-done | bytes 3145744 | tf_op jit(solution)/shard_map/all_gather | solution.py:28
  78.0 2.6 fusion.7
  80.6 62.7 %all-gather.9.cloned.1.call-done = bf16[2048,768]{1,0:T(8,128)(2,1)} async-done(((bf16[128,768]{1,0:T(8,128)(2,1)}), bf16[2048,768]{1,0:T(8,128)(2,1)}) %all-gather.9.cloned.1.call-update) | async-done | bytes 3145744 | tf_op jit(solution)/shard_map/all_gather | solution.py:33
  145.8 67.9 %all-gather.13.cloned.1.call-done = bf16[768,2048]{1,0:T(8,128)(2,1)} async-done(((bf16[768,128]{1,0:T(8,128)(2,1)}), bf16[768,2048]{1,0:T(8,128)(2,1)}) %all-gather.13.cloned.1.call-update) | async-done | bytes 3145744 | tf_op jit(solution)/shard_map/all_gather | solution.py:55
  213.7 4.1 multiply_convert_fusion
  219.0 5.7 all-to-all-start.3
  225.7 7.1 all-to-all-done.3
  232.8 6.1 all-to-all-start.2
  239.3 8.4 %all-to-all-done.2 = bf16[128,16,128]{0,2,1:T(8,128)(2,1)S(1)} async-done(((bf16[128,16,128]{0,2,1:T(8,128)(2,1)}), bf16[128,16,128]{0,2,1:T(8,128)(2,1)S(1)}, u32[]{:S(2)}, u32[]{:S(2)}) %all-to-all-start.2) | async-done | bytes 524320 | tf_op jit(solution)/shard_map/all_to_all | solution.py:48
  248.6 34.6 %all-gather.11.cloned.1.call-done = bf16[2048,768]{1,0:T(8,128)(2,1)} async-done(((bf16[128,768]{1,0:T(8,128)(2,1)}), bf16[2048,768]{1,0:T(8,128)(2,1)}) %all-gather.11.cloned.1.call-update) | async-done | bytes 3145744 | tf_op jit(solution)/shard_map/all_gather | solution.py:37
  283.2 3.7 convolution_multiply_fusion
  286.9 61.5 %all-gather.15.cloned.1.call-done = bf16[2048,768]{1,0:T(8,128)(2,1)} async-done(((bf16[128,768]{1,0:T(8,128)(2,1)}), bf16[2048,768]{1,0:T(8,128)(2,1)}) %all-gather.15.cloned.1.call-update) | async-done | bytes 3145744 | tf_op jit(solution)/shard_map/all_gather | solution.py:60
  348.4 3.9 fusion.10
  352.3 61.3 %all-gather.17.cloned.1.call-done = bf16[2048,768]{1,0:T(8,128)(2,1)} async-done(((bf16[128,768]{1,0:T(8,128)(2,1)}), bf16[2048,768]{1,0:T(8,128)(2,1)}) %all-gather.17.cloned.1.call-update) | async-done | bytes 3145744 | tf_op jit(solution)/shard_map/all_gather | solution.py:61
  413.6 3.9 fusion
  417.6 5.8 all-to-all-start.1
  423.4 2.8 fusion.2
  426.3 4.0 fusion.9
  432.0 6.8 all-to-all-start
  438.9 2.8 fusion.1
  443.7 8.6 %all-to-all-done = f32[16,128,128]{2,1,0:T(8,128)} async-done(((f32[16,128,128]{2,1,0:T(8,128)}), f32[16,128,128]{2,1,0:T(8,128)}, u32[]{:S(2)}, u32[]{:S(2)}) %all-to-all-start) | async-done | bytes 1048608 | tf_op jit(solution)/shard_map/all_to_all | solution.py:39
  455.6 69.1 %reduce-scatter.14.cloned.1.call-done = f32[24,128]{1,0:T(8,128)} async-done(((f32[768,128]{1,0:T(8,128)}), f32[24,128]{1,0:T(8,128)}) %reduce-scatter.14.cloned.1.call-update) | async-done | bytes 12304
  524.7 108.8 %reduce-scatter.10.cloned.1.call-done = f32[128,24]{0,1:T(8,128)} async-done(((f32[128,768]{0,1:T(8,128)}), f32[128,24]{0,1:T(8,128)}) %reduce-scatter.10.cloned.1.call-update) | async-done | bytes 12304
  633.5 108.3 %reduce-scatter.12.cloned.1.call-done = f32[128,24]{0,1:T(8,128)} async-done(((f32[128,768]{0,1:T(8,128)}), f32[128,24]{0,1:T(8,128)}) %reduce-scatter.12.cloned.1.call-update) | async-done | bytes 12304
  (47 shorter events, 18.3 us)
Async XLA Ops:
  7.2 70.8 %all-gather.7.cloned.1.call-start = ((), (), s32[]{:S(2)}) async-start(), calls=%async_computation.7 | async-start | bytes 3342336 | tf_op jit(solution)/shard_map/all_gather | solution.py:28
  7.9 135.4 %all-gather.9.cloned.1.call-start = ((), (), s32[]{:S(2)}) async-start(), calls=%async_computation.8 | async-start | bytes 3342336 | tf_op jit(solution)/shard_map/all_gather | solution.py:33
  8.6 134.6 %copy-start.4 = (bf16[128,2048]{1,0:T(8,128)(2,1)S(1)}, bf16[128,2048]{1,0:T(8,128)(2,1)}, u32[]{:S(2)}) copy-start(bf16[128,2048]{1,0:T(8,128)(2,1)} %param.7) | copy-start | bytes 1572868
  8.7 205.0 %all-gather.13.cloned.1.call-start = ((), (), s32[]{:S(2)}) async-start(), calls=%async_computation.10 | async-start | bytes 3342336 | tf_op jit(solution)/shard_map/all_gather | solution.py:55
  9.4 273.8 %all-gather.11.cloned.1.call-start = ((), (), s32[]{:S(2)}) async-start(), calls=%async_computation.9 | async-start | bytes 3342336 | tf_op jit(solution)/shard_map/all_gather | solution.py:37
  11.4 134.4 %copy-start.2 = (bf16[128,2048]{0,1:T(8,128)(2,1)}, bf16[128,2048]{0,1:T(8,128)(2,1)S(1)}, u32[]{:S(2)}) copy-start(bf16[128,2048]{0,1:T(8,128)(2,1)S(1)} %copy.25) | copy-start | bytes 1572868
  217.8 130.6 %all-gather.15.cloned.1.call-start = ((), (), s32[]{:S(2)}) async-start(), calls=%async_computation.11 | async-start | bytes 3342336 | tf_op jit(solution)/shard_map/all_gather | solution.py:60
  218.4 195.2 %all-gather.17.cloned.1.call-start = ((), (), s32[]{:S(2)}) async-start(), calls=%async_computation.12 | async-start | bytes 3342336 | tf_op jit(solution)/shard_map/all_gather | solution.py:61
  219.0 13.8 %all-to-all-start.3 = ((bf16[128,16,128]{0,2,1:T(8,128)(2,1)}), bf16[128,16,128]{0,2,1:T(8,128)(2,1)S(1)}, u32[]{:S(2)}, u32[]{:S(2)}) async-start(bf16[128,16,128]{0,2,1:T(8,128)(2,1)} %bitcast.11), calls=%async_computation.3 | async-start | bytes 1048576 | tf_op jit(solution)/shard_map/all_to_all | solution.py:49
  232.8 14.8 %all-to-all-start.2 = ((bf16[128,16,128]{0,2,1:T(8,128)(2,1)}), bf16[128,16,128]{0,2,1:T(8,128)(2,1)S(1)}, u32[]{:S(2)}, u32[]{:S(2)}) async-start(bf16[128,16,128]{0,2,1:T(8,128)(2,1)} %bitcast.6), calls=%async_computation.2 | async-start | bytes 1048576 | tf_op jit(solution)/shard_map/all_to_all | solution.py:48
  238.9 285.8 %reduce-scatter.14.cloned.1.call-start = ((), (), s32[]{:S(2)}) async-start(), calls=%async_computation.15 | async-start | bytes 405504
  239.0 109.5 %copy-start.5 = (bf16[128,768]{1,0:T(8,128)(2,1)S(1)}, bf16[128,768]{1,0:T(8,128)(2,1)}, u32[]{:S(2)}) copy-start(bf16[128,768]{1,0:T(8,128)(2,1)} %param.11) | copy-start | bytes 589828
  286.9 126.7 %copy-start.7 = (bf16[128,768]{1,0:T(8,128)(2,1)S(1)}, bf16[128,768]{1,0:T(8,128)(2,1)}, u32[]{:S(2)}) copy-start(bf16[128,768]{1,0:T(8,128)(2,1)} %param.12) | copy-start | bytes 589828
  352.3 71.1 %copy-start.1 = (bf16[2048,768]{1,0:T(8,128)(2,1)S(1)}, bf16[2048,768]{1,0:T(8,128)(2,1)}, u32[]{:S(2)}) copy-start(bf16[2048,768]{1,0:T(8,128)(2,1)} %all-gather.15.cloned.1.call-done) | copy-start | bytes 9437188
  417.6 8.7 %copy-start.6 = (bf16[768,128]{1,0:T(8,128)(2,1)S(1)}, bf16[768,128]{1,0:T(8,128)(2,1)}, u32[]{:S(2)}) copy-start(bf16[768,128]{1,0:T(8,128)(2,1)} %param.13) | copy-start | bytes 589828
  417.6 14.5 %all-to-all-start.1 = ((bf16[16,128,128]{2,1,0:T(8,128)(2,1)}), bf16[16,128,128]{2,1,0:T(8,128)(2,1)}, u32[]{:S(2)}, u32[]{:S(2)}) async-start(bf16[16,128,128]{2,1,0:T(8,128)(2,1)} %bitcast.49), calls=%async_computation.1 | async-start | bytes 1048576 | tf_op jit(solution)/shard_map/all_to_all | solution.py:66
  423.4 210.1 %reduce-scatter.10.cloned.1.call-start = ((), (), s32[]{:S(2)}) async-start(), calls=%async_computation.13 | async-start | bytes 405504
  426.3 12.6 %copy-start = (bf16[2048,768]{1,0:T(8,128)(2,1)S(1)}, bf16[2048,768]{1,0:T(8,128)(2,1)}, u32[]{:S(2)}) copy-start(bf16[2048,768]{1,0:T(8,128)(2,1)} %all-gather.17.cloned.1.call-done) | copy-start | bytes 9437188
  432.0 20.2 %all-to-all-start = ((f32[16,128,128]{2,1,0:T(8,128)}), f32[16,128,128]{2,1,0:T(8,128)}, u32[]{:S(2)}, u32[]{:S(2)}) async-start(f32[16,128,128]{2,1,0:T(8,128)} %bitcast.46), calls=%async_computation | async-start | bytes 2097152 | tf_op jit(solution)/shard_map/all_to_all | solution.py:39
  438.8 302.9 %reduce-scatter.12.cloned.1.call-start = ((), (), s32[]{:S(2)}) async-start(), calls=%async_computation.14 | async-start | bytes 405504
  441.7 12.1 %copy-start.3 = (bf16[128,2048]{0,1:T(8,128)(2,1)S(1)}, bf16[128,2048]{0,1:T(8,128)(2,1)}, u32[]{:S(2)}) copy-start(bf16[128,2048]{0,1:T(8,128)(2,1)} %copy-done.2) | copy-start | bytes 1572868
Sparse Core Ops, SparseCore 0:
  11.0 66.9 all-gather.6
  81.0 62.2 all-gather.8
  146.3 67.3 all-gather.12
  218.0 65.2 all-gather.10
  286.1 62.2 all-gather.14
  351.3 62.2 all-gather.16
  417.0 107.7 reduce-scatter.13
  528.3 105.1 reduce-scatter.9
  636.9 104.8 reduce-scatter.11
where the time goes:
time: 749 us; the launch traced here: 748 us
  waiting for transfers between devices  668 us (89%)
  matrix products  30.3 us (4%)
  starting transfers between devices  24.9 us (3%)
  between operations  14.6 us (2%)
  local copies, waits for them, and re-layouts  8.16 us (1%)
    unnamed x12, waiting for transfers between devices  289 us
    all_gather x1, waiting for transfers between devices, on_device(): lax.all_gather(w_down, 'fsdp', axis=1, tiled=True)  67.9 us
    all_gather x1, waiting for transfers between devices, on_device(): lax.all_gather(w_gate, 'fsdp', axis=0, tiled=True)  65 us
    all_gather x1, waiting for transfers between devices, on_device(): lax.all_gather(w_up, 'fsdp', axis=0, tiled=True)  62.7 us
    all_gather x1, waiting for transfers between devices, on_device(): lax.all_gather(dgate, 'fsdp', axis=0, tiled=True)  61.5 us
    all_gather x1, waiting for transfers between devices, on_device(): lax.all_gather(dup, 'fsdp', axis=0, tiled=True)  61.3 us
    all_gather x1, waiting for transfers between devices, on_device(): hidden_all = lax.all_gather(hidden, 'fsdp', axis=0, tiled=True)  34.6 us
  transfers between devices with their start and end apart: 13, of which 13 were waited for; matrix products, arithmetic and copies ran while one was open for 5% of the time, Pallas kernels for 0%

commit v1 on v0

v1 whole, which is shorter than its diff:
```python
import functools
import math

import jax
import jax.numpy as jnp
from jax import lax
from jax.experimental import pallas as pl
from jax.experimental.pallas import tpu as pltpu
from jax.sharding import PartitionSpec as P

MESH = pl.DeviceIdType.MESH
ROWS = 128
D = 2048
FF = 768
NZ = 16
CHUNKS = 3
PART = 64
BLOCK = 3 * PART
LANES = 128
HALF = BLOCK // 2
F32 = jnp.float32
BF16 = jnp.bfloat16


def dot_nt(left, right):
    return lax.dot_general(left, right, (((1,), (1,)), ((), ())), preferred_element_type=F32)


def dot_nn(left, right):
    return jnp.dot(left, right, preferred_element_type=F32)


def kernel(
    tile, cot, comb, valid, wg, wu, wd,
    out_o, tg_o, cg_o, gr_o,
    wf, wbuf, gbuf, rsib, xbuf, dybuf, weight, hbuf, dgubuf, hT, dguT,
    own, psnd, prcv,
    bsnd, brel, bfin, bacc, asnd, arel, afin, zf, zsnd, zrcv,
    send_sems, recv_sems,
):
    dp = lax.axis_index("dp")
    fs = lax.axis_index("fsdp")
    z, c = dp // 2, dp % 2
    y, x = fs // 4, fs % 4
    h, zh = z % 2, z // 2
    a = x + c * (y - x)
    b = y + c * (x - y)

    def at_ab(aa, bb):
        return (dp, (bb + c * (aa - bb)) * 4 + aa + c * (bb - aa))

    a_r, a_l = at_ab((a + 1) % 4, b), at_ab((a + 3) % 4, b)
    b_r, b_l = at_ab(a, (b + 1) % 4), at_ab(a, (b + 3) % 4)
    sib = (z * 2 + 1 - c, fs)
    pz = (z + 1 - 2 * ((z + c) % 2) + NZ) % NZ
    pair = (pz * 2 + c, fs)
    peers = [((((zh + j) % 8) * 2 + h) * 2 + c, fs) for j in range(1, 8)]

    barrier = pltpu.get_barrier_semaphore()
    everyone = [a_r, a_l, b_r, b_l, sib, pair] + peers
    for dev in everyone:
        pl.semaphore_signal(barrier, inc=1, device_id=dev, device_id_type=MESH)

    copies = {}

    def send(name, src, dst, dev):
        n = len(copies)
        copy = pltpu.make_async_remote_copy(
            src_ref=src, dst_ref=dst, send_sem=send_sems.at[n], recv_sem=recv_sems.at[n],
            device_id=dev, device_id_type=MESH,
        )
        copies[name] = copy
        copy.start()

    def arrived(*name):
        copies[name].wait_recv()

    wf[0] = wg[...].astype(F32).T
    wf[1] = wu[...].astype(F32).T
    wf[2] = wd[...].astype(F32)
    for k in range(CHUNKS):
        for m in range(3):
            rows = [
                wf[m, pl.ds(pl.multiple_of(((t * 2 + h) * 2 + c) * 24 + k * 8, 8), 8), :]
                for t in range(8)
            ]
            wbuf[k, c, b, a, m * PART:(m + 1) * PART, :] = jnp.concatenate(rows, 0).astype(BF16)

    kept = lax.broadcasted_iota(jnp.int32, (ROWS, LANES), 1) < valid[0]
    spread = jnp.broadcast_to(comb[...], (ROWS, LANES))
    weight[0] = jnp.where(kept, spread, 0.0).T
    weight[1] = jnp.where(kept, jnp.ones_like(spread), 0.0).T
    xbuf[0:ROWS, :] = tile[...]
    for s in range(16):
        cols = slice(s * LANES, (s + 1) * LANES)
        dybuf[0:ROWS, cols] = (weight[0] * cot[:, cols].astype(F32)).astype(BF16)

    pl.semaphore_wait(barrier, len(everyone))

    def a_start(k):
        block = wbuf.at[k, c, b, a]
        send(("aR", k), block, block, a_r)
        send(("aL", k), block, block, a_l)

    def a_fwd(k):
        arrived("aR", k)
        block = wbuf.at[k, c, b, (a + 3) % 4, 0:HALF]
        send(("aRR", k), block, block, a_r)
        arrived("aL", k)
        block = wbuf.at[k, c, b, (a + 1) % 4, HALF:BLOCK]
        send(("aLL", k), block, block, a_l)

    def b_start(k):
        arrived("aRR", k)
        arrived("aLL", k)
        slab = wbuf.at[k, c, b]
        send(("bR", k), slab, slab, b_r)
        send(("bL", k), slab, slab, b_l)
        send(("sib0", k), slab, slab, sib)

    def b_fwd(k):
        arrived("bR", k)
        slab = wbuf.at[k, c, (b + 3) % 4]
        send(("bRR", k), slab.at[0:2], slab.at[0:2], b_r)
        send(("sib1", k), slab, slab, sib)
        arrived("bL", k)
        slab = wbuf.at[k, c, (b + 1) % 4]
        send(("bLL", k), slab.at[2:4], slab.at[2:4], b_l)
        send(("sib2", k), slab, slab, sib)

    def b_done(k):
        arrived("bRR", k)
        arrived("bLL", k)
        slab = wbuf.at[k, c, (b + 2) % 4]
        send(("sib3", k), slab, slab, sib)

    def sib_wait(k):
        for i in range(4):
            arrived("sib%d" % i, k)

    def piece(k, m, p, yy, xx):
        at = (k, p, yy, xx) if p == 0 else (k, p, xx, yy)
        return wbuf[at + (slice(m * PART, (m + 1) * PART), slice(None))]

    def wrows(k, m, ys):
        return jnp.concatenate(
            [
                jnp.concatenate([piece(k, m, p, yy, xx) for yy in ys for xx in range(4)], 1)
                for p in range(2)
            ],
            0,
        )

    def hidden_part(k):
        every = range(4)
        w_gu = jnp.concatenate([wrows(k, 0, every), wrows(k, 1, every)], 0)
        gu = dot_nt(xbuf[...], w_gu)
        dh = dot_nt(dybuf[...], wrows(k, 2, every))
        gate, up = gu[:, 0:128], gu[:, 128:256]
        sig = jax.nn.sigmoid(gate)
        hidden = gate * sig * up
        dgate = dh * up * sig * (1.0 + gate * (1.0 - sig))
        dup = dh * gate * sig
        hbuf[:, k * 128:(k + 1) * 128] = hidden.astype(BF16)
        dgubuf[:, k * 256:k * 256 + 128] = dgate.astype(BF16)
        dgubuf[:, k * 256 + 128:(k + 1) * 256] = dup.astype(BF16)
        hT[...] = hidden.T.astype(BF16)
        dguT[0:128, :] = dgate.T.astype(BF16)
        dguT[128:256, :] = dup.T.astype(BF16)

    def grads(k):
        def body(yy, _):
            cols = pl.ds(pl.multiple_of(yy * 512, 512), 512)
            g_gu = dot_nn(dguT[...], xbuf[:, cols])
            g_d = dot_nn(hT[...], dybuf[:, cols])
            for m in range(3):
                for p in range(2):
                    for xx in range(4):
                        at = (k, p, yy, xx) if p == 0 else (k, p, xx, yy)
                        base = p * PART + (m * 128 if m < 2 else 0)
                        g = (g_gu if m < 2 else g_d)[base:base + PART, xx * 128:(xx + 1) * 128]
                        gbuf[at + (slice(m * PART, (m + 1) * PART), slice(None))] = g.astype(BF16)
            return 0

        lax.fori_loop(0, 4, body, 0)
        for i, off in enumerate((2, 1, 3, 0)):
            bb = (a + off) % 4
            send(("gs%d" % i, k), gbuf.at[k, 1 - c, bb], rsib.at[k, bb], sib)

    def project(which):
        def body(yy, _):
            cols = pl.ds(pl.multiple_of(yy * 512, 512), 512)
            if which == 0:
                w = jnp.concatenate([wrows(k, 2, [yy]) for k in range(CHUNKS)], 0)
                res = dot_nn(hbuf[...], w)
            else:
                w = jnp.concatenate(
                    [wrows(k, m, [yy]) for k in range(CHUNKS) for m in range(2)], 0
                )
                res = dot_nn(dgubuf[...], w)
            own[which, :, cols] = res[0:ROWS]
            psnd[which, :, cols] = res[ROWS:2 * ROWS].astype(BF16)
            return 0

        lax.fori_loop(0, 4, body, 0)
        send(("p%d" % which,), psnd.at[which], prcv.at[which], pair)

    def gsum(k, bb, lo, hi):
        return gbuf[k, c, bb, lo:hi].astype(F32) + rsib[k, bb, lo:hi].astype(F32)

    def rb_start(k):
        arrived("gs0", k)
        bsnd[k, 0] = gsum(k, (b + 2) % 4, 0, 4).astype(BF16)
        send(("rbRR", k), bsnd.at[k, 0, 0:2], brel.at[k, 0], b_r)
        send(("rbLL", k), bsnd.at[k, 0, 2:4], brel.at[k, 1], b_l)
        arrived("gs1", k)
        bsnd[k, 1, 2:4] = gsum(k, (b + 1) % 4, 2, 4).astype(BF16)
        send(("rbR0", k), bsnd.at[k, 1, 2:4], bfin.at[k, 0, 2:4], b_r)
        arrived("gs2", k)
        bsnd[k, 2, 0:2] = gsum(k, (b + 3) % 4, 0, 2).astype(BF16)
        send(("rbL0", k), bsnd.at[k, 2, 0:2], bfin.at[k, 1, 0:2], b_l)

    def rb_relay(k):
        arrived("rbRR", k)
        bsnd[k, 1, 0:2] = (gsum(k, (b + 1) % 4, 0, 2) + brel[k, 0].astype(F32)).astype(BF16)
        send(("rbR1", k), bsnd.at[k, 1, 0:2], bfin.at[k, 0, 0:2], b_r)
        arrived("rbLL", k)
        bsnd[k, 2, 2:4] = (gsum(k, (b + 3) % 4, 2, 4) + brel[k, 1].astype(F32)).astype(BF16)
        send(("rbL1", k), bsnd.at[k, 2, 2:4], bfin.at[k, 1, 2:4], b_l)

    def rb_final(k):
        arrived("gs3", k)
        for name in ("rbR0", "rbL0", "rbR1", "rbL1"):
            arrived(name, k)
        bacc[k] = gsum(k, b, 0, 4) + bfin[k, 0].astype(F32) + bfin[k, 1].astype(F32)

    def ra_start(k):
        a2, ar, al = (a + 2) % 4, (a + 1) % 4, (a + 3) % 4
        asnd[k, 0] = bacc[k, a2].astype(BF16)
        send(("raRR", k), asnd.at[k, 0, 0:HALF], arel.at[k, 0], a_r)
        send(("raLL", k), asnd.at[k, 0, HALF:BLOCK], arel.at[k, 1], a_l)
        asnd[k, 1, HALF:BLOCK] = bacc[k, ar, HALF:BLOCK].astype(BF16)
        send(("raR0", k), asnd.at[k, 1, HALF:BLOCK], afin.at[k, 0, HALF:BLOCK], a_r)
        asnd[k, 2, 0:HALF] = bacc[k, al, 0:HALF].astype(BF16)
        send(("raL0", k), asnd.at[k, 2, 0:HALF], afin.at[k, 1, 0:HALF], a_l)

    def ra_relay(k):
        ar, al = (a + 1) % 4, (a + 3) % 4
        arrived("raRR", k)
        asnd[k, 1, 0:HALF] = (bacc[k, ar, 0:HALF] + arel[k, 0].astype(F32)).astype(BF16)
        send(("raR1", k), asnd.at[k, 1, 0:HALF], afin.at[k, 0, 0:HALF], a_r)
        arrived("raLL", k)
        asnd[k, 2, HALF:BLOCK] = (bacc[k, al, HALF:BLOCK] + arel[k, 1].astype(F32)).astype(BF16)
        send(("raL1", k), asnd.at[k, 2, HALF:BLOCK], afin.at[k, 1, HALF:BLOCK], a_l)

    def ra_final(k):
        for name in ("raR0", "raL0", "raR1", "raL1"):
            arrived(name, k)
        blk = bacc[k, a] + afin[k, 0].astype(F32) + afin[k, 1].astype(F32)
        for t in range(8):
            rows = jnp.concatenate([blk[m * PART + t * 8:m * PART + t * 8 + 8] for m in range(3)], 0)
            zf[k, t] = rows
            zsnd[k, t] = jnp.concatenate([rows, jnp.zeros((8, LANES), F32)], 0).astype(BF16)
        for j in range(1, 8):
            send(("z%d" % j, k), zsnd.at[k, (zh + j) % 8], zrcv.at[k, j - 1], peers[j - 1])

    def z_final(k):
        total = zf[k, zh]
        for j in range(1, 8):
            arrived("z%d" % j, k)
            total = total + zrcv[k, j - 1].astype(F32)[0:24]
        total = total * (1.0 / 256.0)
        for m in range(3):
            gr_o[m, k * 8:(k + 1) * 8, :] = total[m * 8:(m + 1) * 8]

    for k in range(CHUNKS):
        a_start(k)
    send(("tile",), xbuf.at[0:ROWS], xbuf.at[ROWS:2 * ROWS], pair)
    send(("dy",), dybuf.at[0:ROWS], dybuf.at[ROWS:2 * ROWS], pair)
    for k in range(CHUNKS):
        a_fwd(k)
    b_start(0)
    b_start(1)
    b_fwd(0)
    b_start(2)
    b_fwd(1)
    b_done(0)
    sib_wait(0)
    arrived("tile")
    arrived("dy")
    hidden_part(0)
    b_fwd(2)
    b_done(1)
    grads(0)
    sib_wait(1)
    hidden_part(1)
    b_done(2)
    grads(1)
    rb_start(0)
    sib_wait(2)
    hidden_part(2)
    grads(2)
    rb_relay(0)
    rb_start(1)
    project(0)
    rb_final(0)
    ra_start(0)
    rb_relay(1)
    rb_start(2)
    project(1)
    ra_relay(0)
    rb_final(1)
    ra_start(1)
    rb_relay(2)
    ra_final(0)
    ra_relay(1)
    rb_final(2)
    ra_start(2)
    ra_final(1)
    ra_relay(2)
    ra_final(2)

    arrived("p0")
    dots = jnp.zeros((ROWS, LANES), F32)
    for s in range(16):
        cols = slice(s * LANES, (s + 1) * LANES)
        full = own[0, :, cols] + prcv[0, :, cols].astype(F32)
        out_o[:, cols] = (weight[0] * full).astype(BF16)
        dots = dots + cot[:, cols].astype(F32) * full
    total = jnp.broadcast_to(jnp.sum(dots, axis=1, keepdims=True), (ROWS, LANES))
    total = total * weight[1] * (1.0 / math.sqrt(D))
    cg_o[...] = total.T[0:1, :]
    arrived("p1")
    for s in range(16):
        cols = slice(s * LANES, (s + 1) * LANES)
        tg_o[:, cols] = (own[1, :, cols] + prcv[1, :, cols].astype(F32)).astype(BF16)
    for k in range(CHUNKS):
        z_final(k)
    for copy in copies.values():
        copy.wait_send()


N_COPIES = 36 + 23 * CHUNKS + 4


def on_device(tile, cotangent, combine, valid, w_gate, w_up, w_down):
    vmem = pl.BlockSpec(memory_space=pltpu.VMEM)
    smem = pl.BlockSpec(memory_space=pltpu.SMEM)
    k = CHUNKS
    out, tg, cg, gr = pl.pallas_call(
        kernel,
        out_shape=(
            jax.ShapeDtypeStruct((ROWS, D), BF16),
            jax.ShapeDtypeStruct((ROWS, D), BF16),
            jax.ShapeDtypeStruct((1, ROWS), F32),
            jax.ShapeDtypeStruct((3, 24, LANES), F32),
        ),
        in_specs=[vmem, vmem, vmem, smem, vmem, vmem, vmem],
        out_specs=(vmem, vmem, vmem, vmem),
        scratch_shapes=[
            pltpu.VMEM((3, FF, LANES), F32),
            pltpu.VMEM((k, 2, 4, 4, BLOCK, LANES), BF16),
            pltpu.VMEM((k, 2, 4, 4, BLOCK, LANES), BF16),
            pltpu.VMEM((k, 4, 4, BLOCK, LANES), BF16),
            pltpu.VMEM((2 * ROWS, D), BF16),
            pltpu.VMEM((2 * ROWS, D), BF16),
            pltpu.VMEM((2, ROWS, LANES), F32),
            pltpu.VMEM((2 * ROWS, k * 128), BF16),
            pltpu.VMEM((2 * ROWS, k * 256), BF16),
            pltpu.VMEM((128, 2 * ROWS), BF16),
            pltpu.VMEM((256, 2 * ROWS), BF16),
            pltpu.VMEM((2, ROWS, D), F32),
            pltpu.VMEM((2, ROWS, D), BF16),
            pltpu.VMEM((2, ROWS, D), BF16),
            pltpu.VMEM((k, 3, 4, BLOCK, LANES), BF16),
            pltpu.VMEM((k, 2, 2, BLOCK, LANES), BF16),
            pltpu.VMEM((k, 2, 4, BLOCK, LANES), BF16),
            pltpu.VMEM((k, 4, BLOCK, LANES), F32),
            pltpu.VMEM((k, 3, BLOCK, LANES), BF16),
            pltpu.VMEM((k, 2, HALF, LANES), BF16),
            pltpu.VMEM((k, 2, BLOCK, LANES), BF16),
            pltpu.VMEM((k, 8, 24, LANES), F32),
            pltpu.VMEM((k, 8, 32, LANES), BF16),
            pltpu.VMEM((k, 7, 32, LANES), BF16),
            pltpu.SemaphoreType.DMA((N_COPIES,)),
            pltpu.SemaphoreType.DMA((N_COPIES,)),
        ],
        compiler_params=pltpu.CompilerParams(
            collective_id=0, has_side_effects=True, vmem_limit_bytes=52 * 1024 * 1024
        ),
        cost_estimate=pl.CostEstimate(
            flops=18 * ROWS * D * FF, bytes_accessed=4 * 1024 * 1024, transcendentals=ROWS * FF
        ),
    )(tile, cotangent, combine.reshape(1, ROWS), valid, w_gate, w_up, w_down)
    return (out, tg, cg.reshape(ROWS), gr[0].T, gr[1].T, gr[2])


def solution(mesh):
    in_specs = (
        P(("dp", "fsdp"), None),
        P(("dp", "fsdp"), None),
        P(("dp", "fsdp")),
        P(("dp", "fsdp")),
        P("fsdp", None),
        P("fsdp", None),
        P(None, "fsdp"),
    )
    out_specs = (
        P(("dp", "fsdp"), None),
        P(("dp", "fsdp"), None),
        P(("dp", "fsdp")),
        P("fsdp", "dp"),
        P("fsdp", "dp"),
        P("dp", "fsdp"),
    )
    return jax.shard_map(
        on_device, mesh=mesh, in_specs=in_specs, out_specs=out_specs, check_vma=False
    )
```

time: 749 us -> 81.5 us (0.11)
  the two profiles are of different devices: /device:TPU:6 before, /device:TPU:2 now
where the time goes in v1:
time: 81.5 us; the launch traced here: 81.3 us
  Pallas kernels  73.9 us (91%)
  local copies, waits for them, and re-layouts  6.13 us (8%)
  between operations  1.3 us (2%)
    pallas_call x1, Pallas kernels, on_device(): pl.pallas_call(kernel, out_shape=(jax.ShapeDtypeStruct((ROWS, D), BF16),...  73.9 us
    unnamed x11, local copies, waits for them, and re-layouts  5.52 us

profile of v1, /device:TPU:2, one launch (start us, length us, event | category | flops | bytes accessed | tf_op | source)
XLA Modules:
  0.0 81.3 jit_solution(10697448007195678477)
XLA Ops:
  1.3 0.0 copy-start.3
  1.3 0.6 copy-done.3
  1.9 0.0 copy-start
  1.9 0.9 %copy-done = bf16[128,768]{1,0:T(8,128)(2,1)S(1)} copy-done((bf16[128,768]{1,0:T(8,128)(2,1)S(1)}, bf16[128,768]{1,0:T(8,128)(2,1)}, u32[]{:S(2)}) %copy-start) | copy-done | bytes 196632
  2.9 0.0 copy-start.1
  2.9 0.9 %copy-done.1 = bf16[128,768]{1,0:T(8,128)(2,1)S(1)} copy-done((bf16[128,768]{1,0:T(8,128)(2,1)S(1)}, bf16[128,768]{1,0:T(8,128)(2,1)}, u32[]{:S(2)}) %copy-start.1) | copy-done | bytes 196632
  3.8 0.0 copy-start.2
  3.8 0.9 %copy-done.2 = bf16[768,128]{1,0:T(8,128)(2,1)S(1)} copy-done((bf16[768,128]{1,0:T(8,128)(2,1)S(1)}, bf16[768,128]{1,0:T(8,128)(2,1)}, u32[]{:S(2)}) %copy-start.2) | copy-done | bytes 196632
  4.7 73.9 %shard_map.118 = (bf16[128,2048]{1,0:T(8,128)(2,1)S(1)}, bf16[128,2048]{1,0:T(8,128)(2,1)S(1)}, f32[1,128]{1,0:T(1,128)S(1)}, f32[3,24,128]{2,1,0:T(8,128)S(1)}) custom-call(bf16[128,2048]{1,0:T(8,128)(2,1)} %tile.1, bf16[128,2048]{1,0:T(8,128)(2,1)} %cot.1, f32[1,128]{1,0:T(1,128)S(1)} %bitcast.12, s32[1]{0:T(128)S(6)} %copy.16.valid, ...), custom_call_target="tpu_custom_call" | custom-call | flops 3623878656 | bytes 4194304 | tf_op jit(solution)/shard_map/pallas_call | solution.py:350
  78.6 0.6 slice_bitcast_fusion
  79.2 0.8 copy.17
  80.0 0.8 copy.18
  80.8 0.5 copy.19
Async XLA Ops:
  1.3 0.7 copy-start.3
  1.9 0.9 %copy-start = (bf16[128,768]{1,0:T(8,128)(2,1)S(1)}, bf16[128,768]{1,0:T(8,128)(2,1)}, u32[]{:S(2)}) copy-start(bf16[128,768]{1,0:T(8,128)(2,1)} %wg.1) | copy-start | bytes 589828
  2.9 0.9 %copy-start.1 = (bf16[128,768]{1,0:T(8,128)(2,1)S(1)}, bf16[128,768]{1,0:T(8,128)(2,1)}, u32[]{:S(2)}) copy-start(bf16[128,768]{1,0:T(8,128)(2,1)} %wu.1) | copy-start | bytes 589828
  3.8 0.9 %copy-start.2 = (bf16[768,128]{1,0:T(8,128)(2,1)S(1)}, bf16[768,128]{1,0:T(8,128)(2,1)}, u32[]{:S(2)}) copy-start(bf16[768,128]{1,0:T(8,128)(2,1)} %wd.1) | copy-start | bytes 589828

commit v2 on v1

v2 whole, which is shorter than its diff:
```python
import functools
import math

import jax
import jax.numpy as jnp
from jax import lax
from jax.experimental import pallas as pl
from jax.experimental.pallas import tpu as pltpu
from jax.sharding import PartitionSpec as P

MESH = pl.DeviceIdType.MESH
ROWS = 128
D = 2048
FF = 768
NZ = 16
N_RELAYED = 0
CHUNKS = 3
PART = 64
BLOCK = 3 * PART
LANES = 128
F32 = jnp.float32
BF16 = jnp.bfloat16


def dot_nt(left, right):
    return lax.dot_general(left, right, (((1,), (1,)), ((), ())), preferred_element_type=F32)


def dot_nn(left, right):
    return jnp.dot(left, right, preferred_element_type=F32)


VMEM_BYTES = 60 * 1024 * 1024


def hand_over(*refs):
    ins, outs, held, sems = refs[:4], refs[4:10], refs[10:14], refs[14]
    loads = [
        pltpu.make_async_copy(src, dst, sems.at[n]) for n, (src, dst) in enumerate(zip(ins, held))
    ]
    parts = [(0, held[0]), (1, held[1]), (2, held[2])] + [(3, held[3].at[m]) for m in range(3)]
    stores = [
        pltpu.make_async_copy(src, dst, sems.at[4 + n])
        for n, ((_, src), dst) in enumerate(zip(parts, outs))
    ]
    for load in loads:
        load.start()
    for n, load in enumerate(loads):
        load.wait()
        for (of, _), store in zip(parts, stores):
            if of == n:
                store.start()
    for store in stores:
        store.wait()


def kernel(
    tile, cot, comb, valid, wg, wu, wd,
    out_o, tg_o, cg_o, gr_o,
    wg_v, wu_v, wd_v, cot_v, comb_v, valid_s,
    wbuf, gbuf, rsib, xbuf, dybuf, weight, hbuf, dgubuf, hT, dguT,
    own, psnd, prcv, fin,
    bsnd, brel, bfin, bacc, asnd, afin, zf, zsnd, zrcv,
    load_sems, store_sems, send_sems, recv_sems,
):
    dp = lax.axis_index("dp")
    fs = lax.axis_index("fsdp")
    z, c = dp // 2, dp % 2
    y, x = fs // 4, fs % 4
    h, zh = z % 2, z // 2
    a = x + c * (y - x)
    b = y + c * (x - y)

    def at_ab(aa, bb):
        return (dp, (bb + c * (aa - bb)) * 4 + aa + c * (bb - aa))

    a_to = [at_ab((a + o) % 4, b) for o in range(4)]
    b_to = [at_ab(a, (b + o) % 4) for o in range(4)]
    sib = (z * 2 + 1 - c, fs)
    pz = (z + 1 - 2 * ((z + c) % 2) + NZ) % NZ
    pair = (pz * 2 + c, fs)
    peers = [((((zh + j) % 8) * 2 + h) * 2 + c, fs) for j in range(1, 8)]

    loads = [
        pltpu.make_async_copy(src, dst, load_sems.at[n])
        for n, (src, dst) in enumerate(
            [
                (wg, wg_v), (wu, wu_v), (wd, wd_v), (comb, comb_v),
                (tile, xbuf.at[0:ROWS]), (cot, cot_v), (valid, valid_s),
            ]
        )
    ]
    for load in loads[0:3]:
        load.start()
    barrier = pltpu.get_barrier_semaphore()
    everyone = a_to[1:] + b_to[1:] + [sib, pair] + peers
    for dev in everyone:
        pl.semaphore_signal(barrier, inc=1, device_id=dev, device_id_type=MESH)
    for load in loads[3:]:
        load.start()

    copies, gone = {}, set()

    def send(name, src, dst, dev):
        n = len(copies)
        copy = pltpu.make_async_remote_copy(
            src_ref=src, dst_ref=dst, send_sem=send_sems.at[n], recv_sem=recv_sems.at[n],
            device_id=dev, device_id_type=MESH,
        )
        copies[name] = copy
        copy.start()

    def arrived(*name):
        copies[name].wait_recv()

    def sent(*names):
        for name in names:
            copies[name].wait_send()
            gone.add(name)

    row = lax.broadcasted_iota(jnp.int32, (CHUNKS * PART, LANES), 0)
    lane = lax.broadcasted_iota(jnp.int32, (CHUNKS * PART, LANES), 1)
    unit = (((row % PART) // 8 * 2 + h) * 2 + c) * 24 + row // PART * 8 + row % 8 - lane
    pick = jnp.concatenate(
        [jnp.where(unit == n * LANES, 1.0, 0.0).astype(BF16) for n in range(FF // LANES)], 1
    )
    for m in range(3):
        loads[m].wait()
        rows = dot_nt(pick, (wg_v, wu_v)[m][...]) if m < 2 else dot_nn(pick, wd_v[...])
        for k in range(CHUNKS):
            wbuf[k, c, b, a, m * PART:(m + 1) * PART, :] = rows[k * PART:(k + 1) * PART].astype(BF16)

    pl.semaphore_wait(barrier, len(everyone))

    def own_start(k):
        block = wbuf.at[k, c, b, a]
        for o in (2, 1, 3):
            send(("a", o, k), block, block, a_to[o])
        for o in (1, 3):
            send(("b", o, 0, k), block, block, b_to[o])

    def slab_start(k):
        for o in (3, 1, 2):
            arrived("a", (4 - o) % 4, k)
            block = wbuf.at[k, c, b, (a + o) % 4]
            for to in (1, 3):
                send(("b", to, o, k), block, block, b_to[to])
        slab = wbuf.at[k, c, b]
        send(("sib0", k), slab, slab, sib)

    def forward(k, to, o):
        arrived("b", to, o, k)
        block = wbuf.at[k, c, (b + 4 - to) % 4, (a + o) % 4]
        send(("f", to, o, k), block, block, b_to[to])

    def slabs_in(k):
        for to in (1, 3):
            for o in ((1, 3) if to == 1 else (0, 2)):
                arrived("b", to, o, k)
            slab = wbuf.at[k, c, (b + 4 - to) % 4]
            send(("sib%d" % to, k), slab, slab, sib)

    def last_slab_in(k):
        for to, o in ((1, 0), (1, 2), (3, 1), (3, 3)):
            arrived("f", to, o, k)
        slab = wbuf.at[k, c, (b + 2) % 4]
        send(("sib2", k), slab, slab, sib)

    def sib_wait(k):
        for i in range(4):
            arrived("sib%d" % i, k)

    def piece(k, m, p, yy, xx):
        at = (k, p, yy, xx) if p == 0 else (k, p, xx, yy)
        return wbuf[at + (slice(m * PART, (m + 1) * PART), slice(None))]

    def wrows(k, m, ys):
        return jnp.concatenate(
            [
                jnp.concatenate([piece(k, m, p, yy, xx) for yy in ys for xx in range(4)], 1)
                for p in range(2)
            ],
            0,
        )

    def hidden_part(k):
        every = range(4)
        w_gu = jnp.concatenate([wrows(k, 0, every), wrows(k, 1, every)], 0)
        gu = dot_nt(xbuf[...], w_gu)
        dh = dot_nt(dybuf[...], wrows(k, 2, every))
        gate, up = gu[:, 0:128], gu[:, 128:256]
        sig = jax.nn.sigmoid(gate)
        hidden = gate * sig * up
        dgate = dh * up * sig * (1.0 + gate * (1.0 - sig))
        dup = dh * gate * sig
        hbuf[:, k * 128:(k + 1) * 128] = hidden.astype(BF16)
        dgubuf[:, k * 256:k * 256 + 128] = dgate.astype(BF16)
        dgubuf[:, k * 256 + 128:(k + 1) * 256] = dup.astype(BF16)
        hT[...] = hidden.T.astype(BF16)
        dguT[0:128, :] = dgate.T.astype(BF16)
        dguT[128:256, :] = dup.T.astype(BF16)

    def grads(k):
        def body(yy, _):
            cols = pl.ds(pl.multiple_of(yy * 512, 512), 512)
            g_gu = dot_nn(dguT[...], xbuf[:, cols])
            g_d = dot_nn(hT[...], dybuf[:, cols])
            for m in range(3):
                for p in range(2):
                    for xx in range(4):
                        at = (k, p, yy, xx) if p == 0 else (k, p, xx, yy)
                        base = p * PART + (m * 128 if m < 2 else 0)
                        g = (g_gu if m < 2 else g_d)[base:base + PART, xx * 128:(xx + 1) * 128]
                        gbuf[at + (slice(m * PART, (m + 1) * PART), slice(None))] = g.astype(BF16)
            return 0

        lax.fori_loop(0, 4, body, 0)

    def grads_send(k):
        for i, off in enumerate((2, 1, 3, 0)):
            bb = (a + off) % 4
            send(("gs%d" % i, k), gbuf.at[k, 1 - c, bb], rsib.at[k, bb], sib)

    def project(which):
        def body(yy, _):
            cols = pl.ds(pl.multiple_of(yy * 512, 512), 512)
            if which == 0:
                w = jnp.concatenate([wrows(k, 2, [yy]) for k in range(CHUNKS)], 0)
                res = dot_nn(hbuf[...], w)
            else:
                w = jnp.concatenate(
                    [wrows(k, m, [yy]) for k in range(CHUNKS) for m in range(2)], 0
                )
                res = dot_nn(dgubuf[...], w)
            own[which, :, cols] = res[0:ROWS]
            psnd[which, :, cols] = res[ROWS:2 * ROWS].astype(BF16)
            return 0

        lax.fori_loop(0, 4, body, 0)

    def pair_send(which):
        send(("p%d" % which,), psnd.at[which], prcv.at[which], pair)

    def gsum(k, bb, i):
        return gbuf[k, c, bb, i].astype(F32) + rsib[k, bb, i].astype(F32)

    def rb_sum(k, o, lo, hi, more=None):
        def body(i, _):
            total = gsum(k, (b + o) % 4, i)
            if more is not None:
                total = total + brel[k, more, i - lo].astype(F32)
            bsnd[k, o - 1, i] = total.astype(BF16)
            return 0

        lax.fori_loop(lo, hi, body, 0)

    def rb_send(k, o, lo, hi):
        part = slice(lo, hi)
        send(("rb", o, lo, k), bsnd.at[k, o - 1, part], bfin.at[k, o - 1, part], b_to[o])

    def rb_start(k):
        arrived("gs0", k)
        rb_sum(k, 2, 0, 4)
        if k < N_RELAYED:
            send(("rr", 1, k), bsnd.at[k, 1, 0:2], brel.at[k, 0], b_to[1])
            send(("rr", 3, k), bsnd.at[k, 1, 2:4], brel.at[k, 1], b_to[3])
        else:
            rb_send(k, 2, 0, 4)
        for i, o in ((1, 1), (2, 3)):
            arrived("gs%d" % i, k)
            lo, hi = ((2, 4) if o == 1 else (0, 2)) if k < N_RELAYED else (0, 4)
            rb_sum(k, o, lo, hi)
            rb_send(k, o, lo, hi)

    def rb_sent(k):
        if k < N_RELAYED:
            sent(("rr", 1, k), ("rr", 3, k), ("rb", 1, 2, k), ("rb", 3, 0, k))
        else:
            sent(*((("rb", o, 0, k)) for o in (1, 2, 3)))

    def rb_relay(k):
        for n, o in enumerate((1, 3)):
            arrived("rr", o, k)
            lo, hi = (0, 2) if o == 1 else (2, 4)
            rb_sum(k, o, lo, hi, n)
            rb_send(k, o, lo, hi)

    def ra_start(k):
        arrived("gs3", k)
        if k < N_RELAYED:
            waits, terms = [(1, 0), (1, 2), (3, 0), (3, 2)], (1, 3)
        else:
            waits, terms = [(1, 0), (3, 0), (2, 0)], (1, 3, 2)
        for o, lo in waits:
            arrived("rb", o, lo, k)
        for o in (2, 1, 3, 0):
            i = (a + o) % 4
            total = gsum(k, b, i)
            for t in terms:
                total = total + bfin[k, t - 1, i].astype(F32)
            if o:
                asnd[k, o - 1] = total.astype(BF16)
                send(("ra", o, k), asnd.at[k, o - 1], afin.at[k, o - 1], a_to[o])
            else:
                bacc[k] = total

    def ra_final(k):
        blk = bacc[k]
        for o in (1, 3, 2):
            arrived("ra", o, k)
            blk = blk + afin[k, o - 1].astype(F32)
        for t in range(8):
            rows = jnp.concatenate([blk[m * PART + t * 8:m * PART + t * 8 + 8] for m in range(3)], 0)
            zf[k, t] = rows
            zsnd[k, t] = jnp.concatenate([rows, jnp.zeros((8, LANES), F32)], 0).astype(BF16)
        for j in (4, 3, 5, 2, 6, 1, 7):
            send(("z%d" % j, k), zsnd.at[k, (zh + j) % 8], zrcv.at[k, j - 1], peers[j - 1])

    def z_final(k):
        total = zf[k, zh]
        for j in range(1, 8):
            arrived("z%d" % j, k)
            total = total + zrcv[k, j - 1].astype(F32)[0:24]
        total = total * (1.0 / 256.0)
        for m in range(3):
            gr_o[m, k * 8:(k + 1) * 8, :] = total[m * 8:(m + 1) * 8]

    def tile_send():
        send(("tile",), tile, xbuf.at[ROWS:2 * ROWS], pair)

    def dy_send():
        loads[3].wait()
        loads[6].wait()
        kept = lax.broadcasted_iota(jnp.int32, (ROWS, LANES), 1) < valid_s[0]
        spread = jnp.broadcast_to(comb_v[...], (ROWS, LANES))
        weight[0] = jnp.where(kept, spread, 0.0).T
        weight[1] = jnp.where(kept, jnp.ones_like(spread), 0.0).T
        loads[5].wait()
        for s in range(16):
            cols = slice(s * LANES, (s + 1) * LANES)
            dybuf[0:ROWS, cols] = (weight[0] * cot_v[:, cols].astype(F32)).astype(BF16)
        send(("dy",), dybuf.at[0:ROWS], dybuf.at[ROWS:2 * ROWS], pair)

    def rows_wait():
        loads[4].wait()
        arrived("tile")
        arrived("dy")

    stores = [
        pltpu.make_async_copy(fin.at[n], ref, store_sems.at[n]) for n, ref in enumerate((out_o, tg_o))
    ]

    def output_final():
        arrived("p0")

        def body(s, dots):
            cols = pl.ds(pl.multiple_of(s * LANES, LANES), LANES)
            full = own[0, :, cols] + prcv[0, :, cols].astype(F32)
            fin[0, :, cols] = (weight[0] * full).astype(BF16)
            return dots + cot_v[:, cols].astype(F32) * full

        dots = lax.fori_loop(0, 16, body, jnp.zeros((ROWS, LANES), F32))
        stores[0].start()
        total = jnp.broadcast_to(jnp.sum(dots, axis=1, keepdims=True), (ROWS, LANES))
        total = total * weight[1] * (1.0 / math.sqrt(D))
        cg_o[...] = total.T[0:1, :]

    def tile_grad_final():
        arrived("p1")

        def body(s, _):
            cols = pl.ds(pl.multiple_of(s * LANES, LANES), LANES)
            fin[1, :, cols] = (own[1, :, cols] + prcv[1, :, cols].astype(F32)).astype(BF16)
            return 0

        lax.fori_loop(0, 16, body, 0)
        stores[1].start()

    tile_send()
    own_start(0)
    dy_send()
    own_start(1)
    slab_start(0)
    forward(0, 1, 0)
    own_start(2)
    slab_start(1)
    forward(0, 3, 1)
    forward(0, 3, 3)
    forward(0, 1, 2)
    slabs_in(0)
    forward(1, 1, 0)
    slab_start(2)
    last_slab_in(0)
    forward(1, 3, 1)
    forward(1, 3, 3)
    forward(1, 1, 2)
    slabs_in(1)
    forward(2, 1, 0)
    rows_wait()
    sib_wait(0)
    hidden_part(0)
    forward(2, 3, 1)
    forward(2, 3, 3)
    forward(2, 1, 2)
    slabs_in(2)
    last_slab_in(1)
    grads(0)
    grads_send(0)
    sib_wait(1)
    hidden_part(1)
    last_slab_in(2)
    rb_start(0)
    grads(1)
    grads_send(1)
    sib_wait(2)
    hidden_part(2)
    grads(2)
    grads_send(2)
    rb_start(1)
    project(0)
    pair_send(0)
    rb_start(2)
    ra_start(0)
    project(1)
    pair_send(1)
    ra_start(1)
    ra_final(0)
    ra_start(2)
    output_final()
    ra_final(1)
    ra_final(2)
    tile_grad_final()
    for k in range(CHUNKS):
        z_final(k)
    for store in stores:
        store.wait()
    sent(*(name for name in copies if name not in gone))


N_COPIES = (19 + 4 + 6 + 7) * CHUNKS + 3 * N_RELAYED + 4


def on_device(tile, cotangent, combine, valid, w_gate, w_up, w_down):
    vmem = pl.BlockSpec(memory_space=pltpu.VMEM)
    hbm = pl.BlockSpec(memory_space=pltpu.HBM)
    k = CHUNKS
    out, tg, cg, gr = pl.pallas_call(
        kernel,
        out_shape=(
            jax.ShapeDtypeStruct((ROWS, D), BF16),
            jax.ShapeDtypeStruct((ROWS, D), BF16),
            jax.ShapeDtypeStruct((1, ROWS), F32),
            jax.ShapeDtypeStruct((3, 24, LANES), F32),
        ),
        in_specs=[hbm] * 7,
        out_specs=(hbm, hbm, vmem, vmem),
        scratch_shapes=[
            pltpu.VMEM((LANES, FF), BF16),
            pltpu.VMEM((LANES, FF), BF16),
            pltpu.VMEM((FF, LANES), BF16),
            pltpu.VMEM((ROWS, D), BF16),
            pltpu.VMEM((1, ROWS), F32),
            pltpu.SMEM((1,), jnp.int32),
            pltpu.VMEM((k, 2, 4, 4, BLOCK, LANES), BF16),
            pltpu.VMEM((k, 2, 4, 4, BLOCK, LANES), BF16),
            pltpu.VMEM((k, 4, 4, BLOCK, LANES), BF16),
            pltpu.VMEM((2 * ROWS, D), BF16),
            pltpu.VMEM((2 * ROWS, D), BF16),
            pltpu.VMEM((2, ROWS, LANES), F32),
            pltpu.VMEM((2 * ROWS, k * 128), BF16),
            pltpu.VMEM((2 * ROWS, k * 256), BF16),
            pltpu.VMEM((128, 2 * ROWS), BF16),
            pltpu.VMEM((256, 2 * ROWS), BF16),
            pltpu.VMEM((2, ROWS, D), F32),
            pltpu.VMEM((2, ROWS, D), BF16),
            pltpu.VMEM((2, ROWS, D), BF16),
            pltpu.VMEM((2, ROWS, D), BF16),
            pltpu.VMEM((k, 3, 4, BLOCK, LANES), BF16),
            pltpu.VMEM((k, 2, 2, BLOCK, LANES), BF16),
            pltpu.VMEM((k, 3, 4, BLOCK, LANES), BF16),
            pltpu.VMEM((k, BLOCK, LANES), F32),
            pltpu.VMEM((k, 3, BLOCK, LANES), BF16),
            pltpu.VMEM((k, 3, BLOCK, LANES), BF16),
            pltpu.VMEM((k, 8, 24, LANES), F32),
            pltpu.VMEM((k, 8, 32, LANES), BF16),
            pltpu.VMEM((k, 7, 32, LANES), BF16),
            pltpu.SemaphoreType.DMA((7,)),
            pltpu.SemaphoreType.DMA((2,)),
            pltpu.SemaphoreType.DMA((N_COPIES,)),
            pltpu.SemaphoreType.DMA((N_COPIES,)),
        ],
        compiler_params=pltpu.CompilerParams(
            collective_id=0, has_side_effects=True, vmem_limit_bytes=VMEM_BYTES
        ),
        cost_estimate=pl.CostEstimate(
            flops=18 * ROWS * D * FF, bytes_accessed=4 * 1024 * 1024, transcendentals=ROWS * FF
        ),
    )(tile, cotangent, combine.reshape(1, ROWS), valid, w_gate, w_up, w_down)
    grad = jax.ShapeDtypeStruct((24, LANES), F32)
    out, tg, cg, gg, gu, gd = pl.pallas_call(
        hand_over,
        out_shape=(
            jax.ShapeDtypeStruct((ROWS, D), BF16),
            jax.ShapeDtypeStruct((ROWS, D), BF16),
            jax.ShapeDtypeStruct((1, ROWS), F32),
            grad, grad, grad,
        ),
        in_specs=[hbm] * 4,
        out_specs=(hbm,) * 6,
        scratch_shapes=[
            pltpu.VMEM((ROWS, D), BF16),
            pltpu.VMEM((ROWS, D), BF16),
            pltpu.VMEM((1, ROWS), F32),
            pltpu.VMEM((3, 24, LANES), F32),
            pltpu.SemaphoreType.DMA((10,)),
        ],
        compiler_params=pltpu.CompilerParams(vmem_limit_bytes=VMEM_BYTES),
    )(out, tg, cg, gr)
    return (out, tg, cg.reshape(ROWS), gg.T, gu.T, gd)


def solution(mesh):
    in_specs = (
        P(("dp", "fsdp"), None),
        P(("dp", "fsdp"), None),
        P(("dp", "fsdp")),
        P(("dp", "fsdp")),
        P("fsdp", None),
        P("fsdp", None),
        P(None, "fsdp"),
    )
    out_specs = (
        P(("dp", "fsdp"), None),
        P(("dp", "fsdp"), None),
        P(("dp", "fsdp")),
        P("fsdp", "dp"),
        P("fsdp", "dp"),
        P("dp", "fsdp"),
    )
    return jax.shard_map(
        on_device, mesh=mesh, in_specs=in_specs, out_specs=out_specs, check_vma=False
    )
```

time: 81.5 us -> 69.7 us (0.86)
  the two profiles are of different devices: /device:TPU:2 before, /device:TPU:32 now
where the time goes in v2:
time: 69.7 us; the launch traced here: 69.5 us
  Pallas kernels  68.2 us (98%)
  between operations  1.29 us (2%)
    pallas_call x1, Pallas kernels, on_device(): pl.pallas_call(kernel, out_shape=(jax.ShapeDtypeStruct((ROWS, D), BF16),...  66.1 us
    pallas_call x1, Pallas kernels, on_device(): pl.pallas_call(hand_over, out_shape=(jax.ShapeDtypeStruct((ROWS, D), BF16...  2.1 us

profile of v2, /device:TPU:32, one launch (start us, length us, event | category | flops | bytes accessed | tf_op | source)
XLA Modules:
  0.0 69.5 jit_solution(16860687682061107631)
XLA Ops:
  1.3 66.1 %shard_map.118 = (bf16[128,2048]{1,0:T(8,128)(2,1)}, bf16[128,2048]{1,0:T(8,128)(2,1)}, f32[1,128]{1,0:T(1,128)}, f32[3,24,128]{2,1,0:T(8,128)}) custom-call(bf16[128,2048]{1,0:T(8,128)(2,1)} %tile.1, bf16[128,2048]{1,0:T(8,128)(2,1)} %cot.1, f32[1,128]{1,0:T(1,128)} %bitcast.6, s32[1]{0:T(128)S(6)} %copy.13.valid, bf16[128,768]{1,0:T(8,128)(2,1)} %wg.1, ...), custom_call_target="tpu_custom_call" | custom-call | flops 3623878656 | bytes 4194304 | tf_op jit(solution)/shard_map/pallas_call | solution.py:447
  67.4 2.1 %shard_map.119 = (bf16[128,2048]{1,0:T(8,128)(2,1)}, bf16[128,2048]{1,0:T(8,128)(2,1)}, f32[1,128]{1,0:T(1,128)}, f32[24,128]{1,0:T(8,128)}, f32[24,128]{1,0:T(8,128)}, /*index=5*/f32[24,128]{1,0:T(8,128)}) custom-call(bf16[128,2048]{1,0:T(8,128)(2,1)} %get-tuple-element.16.refs_0_, bf16[128,2048]{1,0:T(8,128)(2,1)} %get-tuple-element.17.refs_1_, ...), custom_call_target="tpu_custom_call" | custom-call | tf_op jit(solution)/shard_map/pallas_call | solution.py:500

commit v3 on v2

--- a/solution.py
+++ b/solution.py
@@ -101,14 +101,15 @@
 
     copies, gone = {}, set()
 
-    def send(name, src, dst, dev):
-        n = len(copies)
-        copy = pltpu.make_async_remote_copy(
+    def remote(n, src, dst, dev):
+        return pltpu.make_async_remote_copy(
             src_ref=src, dst_ref=dst, send_sem=send_sems.at[n], recv_sem=recv_sems.at[n],
             device_id=dev, device_id_type=MESH,
         )
-        copies[name] = copy
-        copy.start()
+
+    def send(name, src, dst, dev):
+        copies[name] = remote(len(copies), src, dst, dev)
+        copies[name].start()
 
     def arrived(*name):
         copies[name].wait_recv()
@@ -201,25 +202,31 @@
         dguT[128:256, :] = dup.T.astype(BF16)
 
     def grads(k):
-        def body(yy, _):
-            cols = pl.ds(pl.multiple_of(yy * 512, 512), 512)
-            g_gu = dot_nn(dguT[...], xbuf[:, cols])
-            g_d = dot_nn(hT[...], dybuf[:, cols])
+        first = len(copies)
+
+        def to_sibling(i):
+            bb = (a + 2 - i + (i // 2) * (7 - 2 * i)) % 4
+            return bb, remote(first + i, gbuf.at[k, 1 - c, bb], rsib.at[k, bb], sib)
+
+        def body(i, _):
+            bb, copy = to_sibling(i)
+            where = [(bb + (1 - c) * (n - bb), n + (1 - c) * (bb - n)) for n in range(4)]
+            cols = [pl.ds(pl.multiple_of((yy * 4 + xx) * 128, 128), 128) for yy, xx in where]
+            g_gu = dot_nn(dguT[...], jnp.concatenate([xbuf[:, at] for at in cols], 1))
+            g_d = dot_nn(hT[...], jnp.concatenate([dybuf[:, at] for at in cols], 1))
             for m in range(3):
                 for p in range(2):
-                    for xx in range(4):
+                    for n, (yy, xx) in enumerate(where):
                         at = (k, p, yy, xx) if p == 0 else (k, p, xx, yy)
                         base = p * PART + (m * 128 if m < 2 else 0)
-                        g = (g_gu if m < 2 else g_d)[base:base + PART, xx * 128:(xx + 1) * 128]
+                        g = (g_gu if m < 2 else g_d)[base:base + PART, n * 128:(n + 1) * 128]
                         gbuf[at + (slice(m * PART, (m + 1) * PART), slice(None))] = g.astype(BF16)
+            copy.start()
             return 0
 
         lax.fori_loop(0, 4, body, 0)
-
-    def grads_send(k):
-        for i, off in enumerate((2, 1, 3, 0)):
-            bb = (a + off) % 4
-            send(("gs%d" % i, k), gbuf.at[k, 1 - c, bb], rsib.at[k, bb], sib)
+        for i in range(4):
+            copies[("gs%d" % i, k)] = to_sibling(i)[1]
 
     def project(which):
         def body(yy, _):
@@ -405,18 +412,15 @@
     slabs_in(2)
     last_slab_in(1)
     grads(0)
-    grads_send(0)
     sib_wait(1)
     hidden_part(1)
     last_slab_in(2)
     rb_start(0)
     grads(1)
-    grads_send(1)
     sib_wait(2)
     hidden_part(2)
+    rb_start(1)
     grads(2)
-    grads_send(2)
-    rb_start(1)
     project(0)
     pair_send(0)
     rb_start(2)

time: 69.7 us -> 70.2 us (level)
  no operation moved by 1% of the time
where the time goes in v3:
time: 70.2 us; the launch traced here: 70 us
  Pallas kernels  68.8 us (98%)
  between operations  1.29 us (2%)
    pallas_call x1, Pallas kernels, on_device(): pl.pallas_call(kernel, out_shape=(jax.ShapeDtypeStruct((ROWS, D), BF16),...  66.6 us
    pallas_call x1, Pallas kernels, on_device(): pl.pallas_call(hand_over, out_shape=(jax.ShapeDtypeStruct((ROWS, D), BF16...  2.1 us

profile of v3, /device:TPU:32, one launch (start us, length us, event | category | flops | bytes accessed | tf_op | source)
XLA Modules:
  0.0 70.0 jit_solution(704713225475109174)
XLA Ops:
  1.3 66.6 %shard_map.118 = (bf16[128,2048]{1,0:T(8,128)(2,1)}, bf16[128,2048]{1,0:T(8,128)(2,1)}, f32[1,128]{1,0:T(1,128)}, f32[3,24,128]{2,1,0:T(8,128)}) custom-call(bf16[128,2048]{1,0:T(8,128)(2,1)} %tile.1, bf16[128,2048]{1,0:T(8,128)(2,1)} %cot.1, f32[1,128]{1,0:T(1,128)} %bitcast.6, s32[1]{0:T(128)S(6)} %copy.13.valid, bf16[128,768]{1,0:T(8,128)(2,1)} %wg.1, ...), custom_call_target="tpu_custom_call" | custom-call | flops 3623878656 | bytes 4194304 | tf_op jit(solution)/shard_map/pallas_call | solution.py:451
  67.9 2.1 %shard_map.119 = (bf16[128,2048]{1,0:T(8,128)(2,1)}, bf16[128,2048]{1,0:T(8,128)(2,1)}, f32[1,128]{1,0:T(1,128)}, f32[24,128]{1,0:T(8,128)}, f32[24,128]{1,0:T(8,128)}, /*index=5*/f32[24,128]{1,0:T(8,128)}) custom-call(bf16[128,2048]{1,0:T(8,128)(2,1)} %get-tuple-element.16.refs_0_, bf16[128,2048]{1,0:T(8,128)(2,1)} %get-tuple-element.17.refs_1_, ...), custom_call_target="tpu_custom_call" | custom-call | tf_op jit(solution)/shard_map/pallas_call | solution.py:504
